TPU v7x, 1024 devices: a whole 4x8x16 slice. The times are simulated.
1024 devices in a mesh: layer: 4 (over x_hi, core), tok: 256 (over y, z, x_lo).
Axes of the slice: x: 4 (x_hi: 2, x_lo: 2; x = x_hi * 2 + x_lo), y: 8, z: 16, core: 2. Of those that a mesh axis runs over, the one named last changes fastest.
Arguments:
- acts: bfloat16 [4, 65536, 2304], P('layer', 'tok'), may hold values from -6 to 6
- w_enc: bfloat16 [4, 2304, 16384], P('layer', None, 'tok'), may hold values from -0.0625 to 0.0625
- b_enc: float32 [16384], P('tok'), may hold values from -3 to 3
- w_dec: bfloat16 [4, 16384, 2304], P('layer', 'tok'), may hold values from -0.375 to 0.375
- b_dec: float32 [4, 2304], P('layer'), may hold values from -3 to 3
Outputs:
- latents: bfloat16 [65536, 512], P('tok')
- recon: bfloat16 [4, 65536, 2304], P('layer', 'tok')
All inputs are finite; a program needn't handle non-finite values.
Results may differ from a plain program's by a relative error of at most 0.017.
Values may be sent and summed in bfloat16 or wider, within the bound.
A program may use at most 32 MiB of HBM per device.

v0:
```python
import jax
import jax.numpy as jnp
from jax import lax
from jax.sharding import PartitionSpec as P

GROUP = 64
WINDOW = 8


def passed_along(value, axis, steps):
    count = lax.axis_size(axis)
    pairs = [(source, (source + steps) % count) for source in range(count)]
    return lax.ppermute(value, axis, pairs)


def on_device(acts, w_enc, b_enc, w_dec, b_dec):
    held = (w_enc[0], w_dec[0], b_enc)
    pieces = [held]
    current = held
    for step in range(1, WINDOW):
        current = (
            passed_along(current[0], "tok", 1),
            passed_along(current[1], "tok", 1),
            passed_along(current[2].astype(jnp.bfloat16), "tok", 1).astype(jnp.float32),
        )
        pieces.append(current)
    enc_stack = jnp.stack([p[0] for p in pieces])
    dec_stack = jnp.stack([p[1] for p in pieces])
    bias_stack = jnp.stack([p[2] for p in pieces])
    rows = acts[0]
    bias_all = bias_stack.reshape(WINDOW * GROUP)
    enc_cat = jnp.transpose(enc_stack, (1, 0, 2)).reshape(rows.shape[1], WINDOW * GROUP)
    partial_value = jnp.dot(rows, enc_cat, preferred_element_type=jnp.float32)
    pre = lax.psum(partial_value.astype(jnp.bfloat16), "layer").astype(jnp.float32)
    latents = jnp.maximum(pre + bias_all, 0.0).astype(jnp.bfloat16)
    dec_cat = dec_stack.reshape(WINDOW * GROUP, dec_stack.shape[2])
    recon = jnp.dot(latents, dec_cat, preferred_element_type=jnp.float32) + b_dec[0]
    return (latents, recon.astype(jnp.bfloat16)[None])


def solution(mesh):
    return jax.shard_map(
        on_device,
        mesh=mesh,
        in_specs=(
            P("layer", "tok", None),
            P("layer", None, "tok"),
            P("tok"),
            P("layer", "tok", None),
            P("layer", None),
        ),
        out_specs=(P("tok", None), P("layer", "tok", None)),
        check_vma=False,
    )
```

profile of v0, /device:TPU:1, one launch (start us, length us, event | category | flops | bytes accessed | tf_op | source)
XLA Modules:
  0.0 253.6 jit_solution(5543595571269234617)
XLA Ops:
  7.2 4.1 %collective-permute-start = (bf16[2304,64]{0,1:T(8,128)(2,1)}, bf16[2304,64]{0,1:T(8,128)(2,1)}, u32[]{:S(2)}, u32[]{:S(2)}) collective-permute-start(bf16[2304,64]{0,1:T(8,128)(2,1)} %bitcast.69), channel_id=1, source_target_pairs={{0,1},{1,2},{2,3},{3,4},{4,5},{5,6},{6,7},{7,8},{8,9},{9,10},{10,1... | collective-permute-start | bytes 884744 | tf_op jit(solution)/shard_map/ppermute | solution.py:13
  12.5 4.0 %collective-permute-start.7 = (bf16[64]{0:T(256)(128)(2,1)}, bf16[64]{0:T(256)(128)(2,1)S(1)}, u32[]{:S(2)}, u32[]{:S(2)}) collective-permute-start(bf16[64]{0:T(256)(128)(2,1)} %convert_element_type.16), channel_id=1, source_target_pairs={{0,1},{1,2},{2,3},{3,4},{4,5},{5,6},{6,7},{7,8},{8,9},{9,10},{10,1... | collective-permute-start | bytes 392 | tf_op jit(solution)/shard_map/ppermute | solution.py:13
  16.5 3.1 %collective-permute-start.14 = (bf16[64,2304]{1,0:T(8,128)(2,1)}, bf16[64,2304]{1,0:T(8,128)(2,1)}, u32[]{:S(2)}, u32[]{:S(2)}) collective-permute-start(bf16[64,2304]{1,0:T(8,128)(2,1)} %bitcast.70), channel_id=1, source_target_pairs={{0,1},{1,2},{2,3},{3,4},{4,5},{5,6},{6,7},{7,8},{8,9},{9,10},{10,1... | collective-permute-start | bytes 884744 | tf_op jit(solution)/shard_map/ppermute | solution.py:13
  23.0 14.0 %collective-permute-done.7 = bf16[64]{0:T(256)(128)(2,1)S(1)} collective-permute-done((bf16[64]{0:T(256)(128)(2,1)}, bf16[64]{0:T(256)(128)(2,1)S(1)}, u32[]{:S(2)}, u32[]{:S(2)}) %collective-permute-start.7) | collective-permute-done | bytes 160 | tf_op jit(solution)/shard_map/ppermute | solution.py:13
  39.4 6.1 %collective-permute-done.8 = bf16[64]{0:T(256)(128)(2,1)S(1)} collective-permute-done((bf16[64]{0:T(256)(128)(2,1)S(1)}, bf16[64]{0:T(256)(128)(2,1)S(1)}, u32[]{:S(2)}, u32[]{:S(2)}) %collective-permute-start.8) | collective-permute-done | bytes 160 | tf_op jit(solution)/shard_map/ppermute | solution.py:13
  47.9 6.1 %collective-permute-done.9 = bf16[64]{0:T(256)(128)(2,1)S(1)} collective-permute-done((bf16[64]{0:T(256)(128)(2,1)S(1)}, bf16[64]{0:T(256)(128)(2,1)S(1)}, u32[]{:S(2)}, u32[]{:S(2)}) %collective-permute-start.9) | collective-permute-done | bytes 160 | tf_op jit(solution)/shard_map/ppermute | solution.py:13
  56.4 6.0 %collective-permute-done.10 = bf16[64]{0:T(256)(128)(2,1)S(1)} collective-permute-done((bf16[64]{0:T(256)(128)(2,1)S(1)}, bf16[64]{0:T(256)(128)(2,1)S(1)}, u32[]{:S(2)}, u32[]{:S(2)}) %collective-permute-start.10) | collective-permute-done | bytes 160 | tf_op jit(solution)/shard_map/ppermute | solution.py:13
  65.0 6.0 %collective-permute-done.11 = bf16[64]{0:T(256)(128)(2,1)S(1)} collective-permute-done((bf16[64]{0:T(256)(128)(2,1)S(1)}, bf16[64]{0:T(256)(128)(2,1)S(1)}, u32[]{:S(2)}, u32[]{:S(2)}) %collective-permute-start.11) | collective-permute-done | bytes 160 | tf_op jit(solution)/shard_map/ppermute | solution.py:13
  73.4 6.1 %collective-permute-done.12 = bf16[64]{0:T(256)(128)(2,1)S(1)} collective-permute-done((bf16[64]{0:T(256)(128)(2,1)S(1)}, bf16[64]{0:T(256)(128)(2,1)S(1)}, u32[]{:S(2)}, u32[]{:S(2)}) %collective-permute-start.12) | collective-permute-done | bytes 160 | tf_op jit(solution)/shard_map/ppermute | solution.py:13
  82.0 6.0 %collective-permute-done.13 = bf16[64]{0:T(256)(128)(2,1)S(1)} collective-permute-done((bf16[64]{0:T(256)(128)(2,1)S(1)}, bf16[64]{0:T(256)(128)(2,1)S(1)}, u32[]{:S(2)}, u32[]{:S(2)}) %collective-permute-start.13) | collective-permute-done | bytes 160 | tf_op jit(solution)/shard_map/ppermute | solution.py:13
  96.4 5.3 %collective-permute-done.1 = bf16[2304,64]{0,1:T(8,128)(2,1)S(1)} collective-permute-done((bf16[2304,64]{0,1:T(8,128)(2,1)}, bf16[2304,64]{0,1:T(8,128)(2,1)S(1)}, u32[]{:S(2)}, u32[]{:S(2)}) %collective-permute-start.1) | collective-permute-done | bytes 294944 | tf_op jit(solution)/shard_map/ppermute | solution.py:13
  107.4 9.6 %collective-permute-done.2 = bf16[2304,64]{0,1:T(8,128)(2,1)S(1)} collective-permute-done((bf16[2304,64]{0,1:T(8,128)(2,1)S(1)}, bf16[2304,64]{0,1:T(8,128)(2,1)S(1)}, u32[]{:S(2)}, u32[]{:S(2)}) %collective-permute-start.2) | collective-permute-done | bytes 294944 | tf_op jit(solution)/shard_map/ppermute | solution.py:13
  122.6 6.9 %collective-permute-done.3 = bf16[2304,64]{0,1:T(8,128)(2,1)S(1)} collective-permute-done((bf16[2304,64]{0,1:T(8,128)(2,1)S(1)}, bf16[2304,64]{0,1:T(8,128)(2,1)S(1)}, u32[]{:S(2)}, u32[]{:S(2)}) %collective-permute-start.3) | collective-permute-done | bytes 294944 | tf_op jit(solution)/shard_map/ppermute | solution.py:13
  132.2 3.5 %collective-permute-done.17 = bf16[64,2304]{1,0:T(8,128)(2,1)S(1)} collective-permute-done((bf16[64,2304]{1,0:T(8,128)(2,1)S(1)}, bf16[64,2304]{1,0:T(8,128)(2,1)S(1)}, u32[]{:S(2)}, u32[]{:S(2)}) %collective-permute-start.17) | collective-permute-done | bytes 294944 | tf_op jit(solution)/shard_map/ppermute | solution.py:13
  137.6 3.7 %collective-permute-done.4 = bf16[2304,64]{0,1:T(8,128)(2,1)S(1)} collective-permute-done((bf16[2304,64]{0,1:T(8,128)(2,1)S(1)}, bf16[2304,64]{0,1:T(8,128)(2,1)S(1)}, u32[]{:S(2)}, u32[]{:S(2)}) %collective-permute-start.4) | collective-permute-done | bytes 294944 | tf_op jit(solution)/shard_map/ppermute | solution.py:13
  144.0 6.8 %collective-permute-done.18 = bf16[64,2304]{1,0:T(8,128)(2,1)S(1)} collective-permute-done((bf16[64,2304]{1,0:T(8,128)(2,1)S(1)}, bf16[64,2304]{1,0:T(8,128)(2,1)S(1)}, u32[]{:S(2)}, u32[]{:S(2)}) %collective-permute-start.18) | collective-permute-done | bytes 294944 | tf_op jit(solution)/shard_map/ppermute | solution.py:13
  150.8 1.9 collective-permute-start.19
  152.7 4.1 %collective-permute-done.5 = bf16[2304,64]{0,1:T(8,128)(2,1)S(1)} collective-permute-done((bf16[2304,64]{0,1:T(8,128)(2,1)S(1)}, bf16[2304,64]{0,1:T(8,128)(2,1)S(1)}, u32[]{:S(2)}, u32[]{:S(2)}) %collective-permute-start.5) | collective-permute-done | bytes 294944 | tf_op jit(solution)/shard_map/ppermute | solution.py:13
  159.6 5.8 %collective-permute-done.19 = bf16[64,2304]{1,0:T(8,128)(2,1)} collective-permute-done((bf16[64,2304]{1,0:T(8,128)(2,1)S(1)}, bf16[64,2304]{1,0:T(8,128)(2,1)}, u32[]{:S(2)}, u32[]{:S(2)}) %collective-permute-start.19) | collective-permute-done | bytes 294944 | tf_op jit(solution)/shard_map/ppermute | solution.py:13
  168.3 3.4 %collective-permute-done.6 = bf16[2304,64]{0,1:T(8,128)(2,1)S(1)} collective-permute-done((bf16[2304,64]{0,1:T(8,128)(2,1)S(1)}, bf16[2304,64]{0,1:T(8,128)(2,1)S(1)}, u32[]{:S(2)}, u32[]{:S(2)}) %collective-permute-start.6) | collective-permute-done | bytes 294944 | tf_op jit(solution)/shard_map/ppermute | solution.py:13
  172.4 3.2 %fusion.3 = bf16[256,512]{0,1:T(8,128)(2,1)} fusion(bf16[2304,512]{0,1:T(8,128)(2,1)} %bitcast.71, bf16[1,256,2304]{2,1,0:T(8,128)(2,1)S(1)} %copy-done), kind=kOutput, calls=%fused_computation.5 | convolution fusion | flops 604110848 | bytes 3801088 | tf_op jit(solution)/shard_map/dot_general | solution.py:33
  175.6 3.8 %collective-permute-done.20 = bf16[64,2304]{1,0:T(8,128)(2,1)} collective-permute-done((bf16[64,2304]{1,0:T(8,128)(2,1)}, bf16[64,2304]{1,0:T(8,128)(2,1)}, u32[]{:S(2)}, u32[]{:S(2)}) %collective-permute-start.20) | collective-permute-done | bytes 294944 | tf_op jit(solution)/shard_map/ppermute | solution.py:13
  180.4 60.1 %all-reduce.2.cloned.1.call-done = bf16[256,512]{0,1:T(8,128)(2,1)} async-done(((bf16[256,512]{0,1:T(8,128)(2,1)}), bf16[256,512]{0,1:T(8,128)(2,1)}) %all-reduce.2.cloned.1.call-update) | async-done | bytes 262160 | tf_op jit(solution)/shard_map/psum | solution.py:34
  244.0 2.8 %fusion.1 = bf16[1,256,2304]{2,1,0:T(8,128)(2,1)} fusion(bf16[256,512]{0,1:T(8,128)(2,1)} %maximum_convert_fusion, bf16[512,2304]{1,0:T(8,128)(2,1)S(1)} %bitcast.68, f32[2304]{0:T(1024)S(1)} %reduce), kind=kOutput, calls=%fused_computation.2 | convolution fusion | flops 605159424 | bytes 3810304 | tf_op jit(solution)/shard_map/dot_general | solution.py:37
  (56 shorter events, 57.0 us)
Async XLA Ops:
  7.2 165.2 %copy-start = (bf16[1,256,2304]{2,1,0:T(8,128)(2,1)S(1)}, bf16[1,256,2304]{2,1,0:T(8,128)(2,1)}, u32[]{:S(2)}) copy-start(bf16[1,256,2304]{2,1,0:T(8,128)(2,1)} %param.5) | copy-start | bytes 3538948
  7.2 233.2 %all-reduce.2.cloned.1.call-start = ((), (), s32[]{:S(2)}) async-start(), calls=%async_computation | async-start | bytes 524288 | tf_op jit(solution)/shard_map/psum | solution.py:34
  7.2 82.7 %collective-permute-start = (bf16[2304,64]{0,1:T(8,128)(2,1)}, bf16[2304,64]{0,1:T(8,128)(2,1)}, u32[]{:S(2)}, u32[]{:S(2)}) collective-permute-start(bf16[2304,64]{0,1:T(8,128)(2,1)} %bitcast.69), channel_id=1, source_target_pairs={{0,1},{1,2},{2,3},{3,4},{4,5},{5,6},{6,7},{7,8},{8,9},{9,10},{10,1... | collective-permute-start | bytes 884744 | tf_op jit(solution)/shard_map/ppermute | solution.py:13
  12.5 24.5 %collective-permute-start.7 = (bf16[64]{0:T(256)(128)(2,1)}, bf16[64]{0:T(256)(128)(2,1)S(1)}, u32[]{:S(2)}, u32[]{:S(2)}) collective-permute-start(bf16[64]{0:T(256)(128)(2,1)} %convert_element_type.16), channel_id=1, source_target_pairs={{0,1},{1,2},{2,3},{3,4},{4,5},{5,6},{6,7},{7,8},{8,9},{9,10},{10,1... | collective-permute-start | bytes 392 | tf_op jit(solution)/shard_map/ppermute | solution.py:13
  16.5 77.1 %collective-permute-start.14 = (bf16[64,2304]{1,0:T(8,128)(2,1)}, bf16[64,2304]{1,0:T(8,128)(2,1)}, u32[]{:S(2)}, u32[]{:S(2)}) collective-permute-start(bf16[64,2304]{1,0:T(8,128)(2,1)} %bitcast.70), channel_id=1, source_target_pairs={{0,1},{1,2},{2,3},{3,4},{4,5},{5,6},{6,7},{7,8},{8,9},{9,10},{10,1... | collective-permute-start | bytes 884744 | tf_op jit(solution)/shard_map/ppermute | solution.py:13
  37.0 8.5 %collective-permute-start.8 = (bf16[64]{0:T(256)(128)(2,1)S(1)}, bf16[64]{0:T(256)(128)(2,1)S(1)}, u32[]{:S(2)}, u32[]{:S(2)}) collective-permute-start(bf16[64]{0:T(256)(128)(2,1)S(1)} %collective-permute-done.7), channel_id=1, source_target_pairs={{0,1},{1,2},{2,3},{3,4},{4,5},{5,6},{6,7},{7,8},{8,9},{9,10},{10,1... | collective-permute-start | bytes 392 | tf_op jit(solution)/shard_map/ppermute | solution.py:13
  45.5 8.5 %collective-permute-start.9 = (bf16[64]{0:T(256)(128)(2,1)S(1)}, bf16[64]{0:T(256)(128)(2,1)S(1)}, u32[]{:S(2)}, u32[]{:S(2)}) collective-permute-start(bf16[64]{0:T(256)(128)(2,1)S(1)} %collective-permute-done.8), channel_id=1, source_target_pairs={{0,1},{1,2},{2,3},{3,4},{4,5},{5,6},{6,7},{7,8},{8,9},{9,10},{10,1... | collective-permute-start | bytes 392 | tf_op jit(solution)/shard_map/ppermute | solution.py:13
  54.0 8.5 %collective-permute-start.10 = (bf16[64]{0:T(256)(128)(2,1)S(1)}, bf16[64]{0:T(256)(128)(2,1)S(1)}, u32[]{:S(2)}, u32[]{:S(2)}) collective-permute-start(bf16[64]{0:T(256)(128)(2,1)S(1)} %collective-permute-done.9), channel_id=1, source_target_pairs={{0,1},{1,2},{2,3},{3,4},{4,5},{5,6},{6,7},{7,8},{8,9},{9,10},{10,1... | collective-permute-start | bytes 392 | tf_op jit(solution)/shard_map/ppermute | solution.py:13
  62.5 8.5 %collective-permute-start.11 = (bf16[64]{0:T(256)(128)(2,1)S(1)}, bf16[64]{0:T(256)(128)(2,1)S(1)}, u32[]{:S(2)}, u32[]{:S(2)}) collective-permute-start(bf16[64]{0:T(256)(128)(2,1)S(1)} %collective-permute-done.10), channel_id=1, source_target_pairs={{0,1},{1,2},{2,3},{3,4},{4,5},{5,6},{6,7},{7,8},{8,9},{9,10},{10,1... | collective-permute-start | bytes 392 | tf_op jit(solution)/shard_map/ppermute | solution.py:13
  71.0 8.5 %collective-permute-start.12 = (bf16[64]{0:T(256)(128)(2,1)S(1)}, bf16[64]{0:T(256)(128)(2,1)S(1)}, u32[]{:S(2)}, u32[]{:S(2)}) collective-permute-start(bf16[64]{0:T(256)(128)(2,1)S(1)} %collective-permute-done.11), channel_id=1, source_target_pairs={{0,1},{1,2},{2,3},{3,4},{4,5},{5,6},{6,7},{7,8},{8,9},{9,10},{10,1... | collective-permute-start | bytes 392 | tf_op jit(solution)/shard_map/ppermute | solution.py:13
  79.5 8.5 %collective-permute-start.13 = (bf16[64]{0:T(256)(128)(2,1)S(1)}, bf16[64]{0:T(256)(128)(2,1)S(1)}, u32[]{:S(2)}, u32[]{:S(2)}) collective-permute-start(bf16[64]{0:T(256)(128)(2,1)S(1)} %collective-permute-done.12), channel_id=1, source_target_pairs={{0,1},{1,2},{2,3},{3,4},{4,5},{5,6},{6,7},{7,8},{8,9},{9,10},{10,1... | collective-permute-start | bytes 392 | tf_op jit(solution)/shard_map/ppermute | solution.py:13
  89.9 11.9 %collective-permute-start.1 = (bf16[2304,64]{0,1:T(8,128)(2,1)}, bf16[2304,64]{0,1:T(8,128)(2,1)S(1)}, u32[]{:S(2)}, u32[]{:S(2)}) collective-permute-start(bf16[2304,64]{0,1:T(8,128)(2,1)} %collective-permute-done), channel_id=1, source_target_pairs={{0,1},{1,2},{2,3},{3,4},{4,5},{5,6},{6,7},{7,8},{8,9},{9,10},{10,1... | collective-permute-start | bytes 884744 | tf_op jit(solution)/shard_map/ppermute | solution.py:13
  93.5 11.9 %collective-permute-start.15 = (bf16[64,2304]{1,0:T(8,128)(2,1)}, bf16[64,2304]{1,0:T(8,128)(2,1)S(1)}, u32[]{:S(2)}, u32[]{:S(2)}) collective-permute-start(bf16[64,2304]{1,0:T(8,128)(2,1)} %collective-permute-done.14), channel_id=1, source_target_pairs={{0,1},{1,2},{2,3},{3,4},{4,5},{5,6},{6,7},{7,8},{8,9},{9,10},{10,1... | collective-permute-start | bytes 884744 | tf_op jit(solution)/shard_map/ppermute | solution.py:13
  101.8 15.2 %collective-permute-start.2 = (bf16[2304,64]{0,1:T(8,128)(2,1)S(1)}, bf16[2304,64]{0,1:T(8,128)(2,1)S(1)}, u32[]{:S(2)}, u32[]{:S(2)}) collective-permute-start(bf16[2304,64]{0,1:T(8,128)(2,1)S(1)} %collective-permute-done.1), channel_id=1, source_target_pairs={{0,1},{1,2},{2,3},{3,4},{4,5},{5,6},{6,7},{7,8},{8,9},{9,10},{10,1... | collective-permute-start | bytes 884744 | tf_op jit(solution)/shard_map/ppermute | solution.py:13
  105.4 15.3 %collective-permute-start.16 = (bf16[64,2304]{1,0:T(8,128)(2,1)S(1)}, bf16[64,2304]{1,0:T(8,128)(2,1)S(1)}, u32[]{:S(2)}, u32[]{:S(2)}) collective-permute-start(bf16[64,2304]{1,0:T(8,128)(2,1)S(1)} %collective-permute-done.15), channel_id=1, source_target_pairs={{0,1},{1,2},{2,3},{3,4},{4,5},{5,6},{6,7},{7,8},{8,9},{9,10},{10,1... | collective-permute-start | bytes 884744 | tf_op jit(solution)/shard_map/ppermute | solution.py:13
  117.0 12.5 %collective-permute-start.3 = (bf16[2304,64]{0,1:T(8,128)(2,1)S(1)}, bf16[2304,64]{0,1:T(8,128)(2,1)S(1)}, u32[]{:S(2)}, u32[]{:S(2)}) collective-permute-start(bf16[2304,64]{0,1:T(8,128)(2,1)S(1)} %collective-permute-done.2), channel_id=1, source_target_pairs={{0,1},{1,2},{2,3},{3,4},{4,5},{5,6},{6,7},{7,8},{8,9},{9,10},{10,1... | collective-permute-start | bytes 884744 | tf_op jit(solution)/shard_map/ppermute | solution.py:13
  120.7 15.0 %collective-permute-start.17 = (bf16[64,2304]{1,0:T(8,128)(2,1)S(1)}, bf16[64,2304]{1,0:T(8,128)(2,1)S(1)}, u32[]{:S(2)}, u32[]{:S(2)}) collective-permute-start(bf16[64,2304]{1,0:T(8,128)(2,1)S(1)} %collective-permute-done.16), channel_id=1, source_target_pairs={{0,1},{1,2},{2,3},{3,4},{4,5},{5,6},{6,7},{7,8},{8,9},{9,10},{10,1... | collective-permute-start | bytes 884744 | tf_op jit(solution)/shard_map/ppermute | solution.py:13
  129.5 11.8 %collective-permute-start.4 = (bf16[2304,64]{0,1:T(8,128)(2,1)S(1)}, bf16[2304,64]{0,1:T(8,128)(2,1)S(1)}, u32[]{:S(2)}, u32[]{:S(2)}) collective-permute-start(bf16[2304,64]{0,1:T(8,128)(2,1)S(1)} %collective-permute-done.3), channel_id=1, source_target_pairs={{0,1},{1,2},{2,3},{3,4},{4,5},{5,6},{6,7},{7,8},{8,9},{9,10},{10,1... | collective-permute-start | bytes 884744 | tf_op jit(solution)/shard_map/ppermute | solution.py:13
  135.7 15.1 %collective-permute-start.18 = (bf16[64,2304]{1,0:T(8,128)(2,1)S(1)}, bf16[64,2304]{1,0:T(8,128)(2,1)S(1)}, u32[]{:S(2)}, u32[]{:S(2)}) collective-permute-start(bf16[64,2304]{1,0:T(8,128)(2,1)S(1)} %collective-permute-done.17), channel_id=1, source_target_pairs={{0,1},{1,2},{2,3},{3,4},{4,5},{5,6},{6,7},{7,8},{8,9},{9,10},{10,1... | collective-permute-start | bytes 884744 | tf_op jit(solution)/shard_map/ppermute | solution.py:13
  141.3 15.6 %collective-permute-start.5 = (bf16[2304,64]{0,1:T(8,128)(2,1)S(1)}, bf16[2304,64]{0,1:T(8,128)(2,1)S(1)}, u32[]{:S(2)}, u32[]{:S(2)}) collective-permute-start(bf16[2304,64]{0,1:T(8,128)(2,1)S(1)} %collective-permute-done.4), channel_id=1, source_target_pairs={{0,1},{1,2},{2,3},{3,4},{4,5},{5,6},{6,7},{7,8},{8,9},{9,10},{10,1... | collective-permute-start | bytes 884744 | tf_op jit(solution)/shard_map/ppermute | solution.py:13
  150.8 14.6 %collective-permute-start.19 = (bf16[64,2304]{1,0:T(8,128)(2,1)S(1)}, bf16[64,2304]{1,0:T(8,128)(2,1)}, u32[]{:S(2)}, u32[]{:S(2)}) collective-permute-start(bf16[64,2304]{1,0:T(8,128)(2,1)S(1)} %collective-permute-done.18), channel_id=1, source_target_pairs={{0,1},{1,2},{2,3},{3,4},{4,5},{5,6},{6,7},{7,8},{8,9},{9,10},{10,1... | collective-permute-start | bytes 884744 | tf_op jit(solution)/shard_map/ppermute | solution.py:13
  156.9 14.8 %collective-permute-start.6 = (bf16[2304,64]{0,1:T(8,128)(2,1)S(1)}, bf16[2304,64]{0,1:T(8,128)(2,1)S(1)}, u32[]{:S(2)}, u32[]{:S(2)}) collective-permute-start(bf16[2304,64]{0,1:T(8,128)(2,1)S(1)} %collective-permute-done.5), channel_id=1, source_target_pairs={{0,1},{1,2},{2,3},{3,4},{4,5},{5,6},{6,7},{7,8},{8,9},{9,10},{10,1... | collective-permute-start | bytes 884744 | tf_op jit(solution)/shard_map/ppermute | solution.py:13
  165.4 14.0 %collective-permute-start.20 = (bf16[64,2304]{1,0:T(8,128)(2,1)}, bf16[64,2304]{1,0:T(8,128)(2,1)}, u32[]{:S(2)}, u32[]{:S(2)}) collective-permute-start(bf16[64,2304]{1,0:T(8,128)(2,1)} %collective-permute-done.19), channel_id=1, source_target_pairs={{0,1},{1,2},{2,3},{3,4},{4,5},{5,6},{6,7},{7,8},{8,9},{9,10},{10,1... | collective-permute-start | bytes 884744 | tf_op jit(solution)/shard_map/ppermute | solution.py:13
  172.4 68.0 %copy-start.1 = (f32[512]{0:T(512)S(1)}, f32[512]{0:T(512)}, u32[]{:S(2)}) copy-start(f32[512]{0:T(512)} %add.22) | copy-start | bytes 6148
Sparse Core Ops, SparseCore 0:
  175.7 64.6 all-reduce.1
where the time goes:
time: 255 us; the launch traced here: 254 us
  waiting for transfers between devices  165 us (65%)
  starting transfers between devices  45.6 us (18%)
  local copies, waits for them, and re-layouts  15.1 us (6%)
  between operations  14.3 us (6%)
  other arithmetic  7.43 us (3%)
  matrix products  5.95 us (2%)
    ppermute x21, waiting for transfers between devices, passed_along(): return lax.ppermute(value, axis, pairs)  105 us
    psum x1, waiting for transfers between devices, on_device(): lax.psum(partial_value.astype(jnp.bfloat16), 'layer').astype(jnp.float32)  60.1 us
    ppermute x21, starting transfers between devices, passed_along(): return lax.ppermute(value, axis, pairs)  45.5 us
    unnamed x19, local copies, waits for them, and re-layouts  12 us
  transfers between devices with their start and end apart: 22, of which 20 were waited for; matrix products, arithmetic and copies ran while one was open for 9% of the time, Pallas kernels for 0%

commit v1 on v0

v1 whole, which is shorter than its diff:
```python
import functools

import jax
import jax.numpy as jnp
from jax import lax
from jax.experimental import pallas as pl
from jax.experimental.pallas import tpu as pltpu
from jax.sharding import PartitionSpec as P

GROUP = 64
WINDOW = 8
MESH = pl.DeviceIdType.MESH


def chunk_plan(half):
    widths = [384, 384, 256, 128] if half == 1152 else [half]
    plan, at = [], 0
    for width in widths:
        plan.append((at, width))
        at += width
    return plan


def sem_plan(chunks):
    sizes = dict(enc=9, decx=2, dec=4 * chunks, acts=2, bias=5, bdec=2, sib=1,
                 part=3, gather=3, lat=4, rec=2 * chunks, out=1)
    at, plan = 0, {}
    for name, size in sizes.items():
        plan[name] = at
        at += size
    return plan, at


def kernel(ring, acts, enc, bias, dec, bdec, lat_out, rec_out,
           acts_all, enc_all, dec_all, bias_all, bd_all, pre, total, sib_out, sib_in,
           part_out, part_in, lat, rec, send, recv):
    rows, width = acts.shape
    half = width // 2
    quarter = rows // 4
    window = WINDOW * GROUP
    plan = chunk_plan(half)
    base, _ = sem_plan(len(plan))

    layer = lax.axis_index("layer")
    tok = lax.axis_index("tok")
    g, h = layer // 2, layer % 2
    m2, s = tok - tok % 2, tok % 2
    chip = 2 * g + s
    oh, os = 1 - h, 1 - s
    alone = h == s

    def at_site(g_, h_, s_):
        return (2 * g_ + h_, m2 + s_)

    following = (layer, lax.rem(tok + 2, ring))
    before = (layer, lax.rem(tok + ring - 2, ring))
    sibling = at_site(g, oh, s)

    pending = []

    def remote(src, dst, target, sem):
        return pltpu.make_async_remote_copy(
            src_ref=src, dst_ref=dst, send_sem=send.at[len(pending)], recv_sem=recv.at[sem],
            device_id=target, device_id_type=MESH)

    def push(src, dst, target, sem):
        copy = remote(src, dst, target, sem)
        copy.start()
        pending.append((None, copy))

    def push_or_keep(src, dst, target, sem, keep):
        away = jnp.logical_not(keep)
        copy = remote(src, dst, target, sem)

        @pl.when(away)
        def _():
            copy.start()

        @pl.when(keep)
        def _():
            pltpu.make_async_copy(src, dst, recv.at[sem]).start()

        pending.append((away, copy))

    def arrived(dst, sem):
        pltpu.make_async_copy(dst, dst, recv.at[sem]).wait()

    def lanes(d):
        return pl.ds(pl.multiple_of(d * half, half), half)

    def block(b, count=1):
        if isinstance(b, int):
            return pl.ds(b * GROUP, count * GROUP)
        return pl.ds(pl.multiple_of(b * GROUP, GROUP), count * GROUP)

    own_bias = bias[...]
    bias_all[os] = jnp.broadcast_to(jnp.concatenate([own_bias, own_bias], axis=1), (8, 2 * GROUP))

    barrier = pltpu.get_barrier_semaphore()
    me = 2 * chip + h
    for j in range(1, 8):
        other = lax.rem(me + j, 8)
        pl.semaphore_signal(barrier, inc=1, device_id=at_site(other // 4, other % 2, (other // 2) % 2),
                            device_id_type=MESH)
    for other in (following, before):
        pl.semaphore_signal(barrier, inc=1, device_id=other, device_id_type=MESH)
    pl.semaphore_wait(barrier, 9)

    def exchange(src, dst, sem):
        push(src.at[:, lanes(oh)], dst, at_site(g, oh, h), sem)
        push_or_keep(src.at[:, lanes(h)], dst, at_site(g, h, h), sem, alone)

    exchange(enc, enc_all.at[block(os)], base["enc"] + os)
    push(bias_all.at[os], bias_all.at[os], at_site(g, h, os), base["bias"])

    def enc_wait(b):
        arrived(enc_all.at[block(b)], base["enc"] + b)

    def enc_send(b):
        push(enc_all.at[block(b)], enc_all.at[block(b + 2)], following, base["enc"] + b + 2)

    def bias_pass(i):
        if i == 0:
            arrived(bias_all.at[s], base["bias"])
        else:
            arrived(bias_all.at[pl.ds(2 * i, 2)], base["bias"] + i)
        count = 1 if i == 3 else 2
        push(bias_all.at[pl.ds(2 * i, count)], bias_all.at[pl.ds(2 * i + 2, count)], following,
             base["bias"] + i + 1)

    enc_wait(os)
    enc_send(os)
    enc_wait(s)
    enc_send(s)
    bias_pass(0)

    exchange(dec, dec_all.at[block(os)], base["decx"] + s)
    exchange(acts, acts_all.at[s], base["acts"] + s)
    push(bdec.at[:, lanes(oh)], bd_all.at[1], sibling, base["bdec"] + 1)
    pltpu.make_async_copy(bdec.at[:, lanes(h)], bd_all.at[0], recv.at[base["bdec"]]).start()

    for i in (1, 2):
        for b in (2 * i + os, 2 * i + s):
            enc_wait(b)
            enc_send(b)
        bias_pass(i)
    enc_wait(6)
    enc_send(6)
    bias_pass(3)

    def dec_part(b, count, c):
        off, wide = plan[c]
        return dec_all.at[pl.ds(b * GROUP, count * GROUP), pl.ds(off, wide)]

    def dec_sem(c, i):
        return base["dec"] + 4 * c + i - 1

    def dec_send(i, c):
        if i > 0:
            arrived(dec_part(2 * i, 2, c), dec_sem(c, i))
        count = 1 if i == 3 else 2
        push(dec_part(2 * i, count, c), dec_part(2 * i + 2, count, c), following, dec_sem(c, i + 1))

    for p in (0, 1):
        arrived(dec_all.at[block(1 - p)], base["decx"] + p)
    for c in range(len(plan)):
        dec_send(0, c)

    arrived(acts_all.at[0], base["acts"])
    arrived(acts_all.at[1], base["acts"] + 1)

    def encode(t, q):
        first = (1 - t) * GROUP + q * (window // 2)
        pre[t, :, q * (window // 2):(q + 1) * (window // 2)] = lax.dot_general(
            acts_all[t], enc_all[first:first + window // 2, :], (((1,), (1,)), ((), ())),
            preferred_element_type=jnp.float32)

    steps = [(i, c) for c in range(len(plan)) for i in (1, 2, 3)]
    steps.sort(key=lambda step: (step[0] + step[1], step[1]))
    done = []

    def pass_on(count):
        for _ in range(count):
            if steps:
                step = steps.pop(0)
                dec_send(*step)
                done.append(step)

    encode(1, 0)
    encode(0, 0)
    enc_wait(7)
    encode(1, 1)
    enc_wait(8)
    encode(0, 1)

    sib_out[...] = pre[oh].astype(jnp.bfloat16)
    push(sib_out, sib_in, sibling, base["sib"])
    pass_on(2)
    arrived(sib_in, base["sib"])
    total[...] = pre[h] + sib_in[...].astype(jnp.float32)
    part_out[...] = total[...].astype(jnp.bfloat16)

    def chip_rows(c_):
        return pl.ds(pl.multiple_of(c_ * quarter, quarter), quarter)

    for j in (1, 3, 2):
        other = lax.rem(chip + j, 4)
        push(part_out.at[chip_rows(other)], part_in.at[j - 1], at_site(other // 2, h, other % 2),
             base["part"] + j - 1)
    pass_on(2)
    arrived(bias_all.at[pl.ds(8, 1)], base["bias"] + 4)
    low = lax.broadcasted_iota(jnp.int32, (1, 2 * GROUP), 1) < GROUP
    first = 1 - h
    bias_row = jnp.concatenate(
        [jnp.where(low, bias_all[first + k, 0:1, :], bias_all[first + k + 1, 0:1, :])
         for k in range(0, WINDOW, 2)], axis=1)
    for j in (1, 2, 3):
        arrived(part_in.at[j - 1], base["part"] + j - 1)
    value = total[chip_rows(chip), :] + bias_row
    for j in (1, 2, 3):
        value = value + part_in[j - 1].astype(jnp.float32)
    lat[h, chip_rows(chip), :] = jnp.maximum(value, 0.0).astype(jnp.bfloat16)

    mine = lat.at[h, chip_rows(chip)]
    for j in (1, 3, 2):
        other = lax.rem(chip + j, 4)
        push(mine, mine, at_site(other // 2, h, other % 2), base["gather"] + j - 1)
    push(mine, mine, sibling, base["lat"])
    pass_on(3)
    for j in (1, 3, 2):
        piece = lat.at[h, chip_rows(lax.rem(chip + 4 - j, 4))]
        arrived(piece, base["gather"] + j - 1)
        push(piece, piece, sibling, base["lat"] + j)
    pass_on(1)
    for j in (0, 1, 3, 2):
        arrived(lat.at[oh, chip_rows(lax.rem(chip + 4 - j, 4))], base["lat"] + j)
    latents_copy = pltpu.make_async_copy(lat.at[s], lat_out, recv.at[base["out"]])
    latents_copy.start()

    arrived(bd_all.at[0], base["bdec"])
    arrived(bd_all.at[1], base["bdec"] + 1)
    shift = jnp.where(alone, bd_all[0], bd_all[1])

    def decode(c):
        off, wide = plan[c]
        while (3, c) not in done:
            pass_on(1)
        arrived(dec_part(8, 1, c), dec_sem(c, 4))
        for t in (0, 1):
            first = (1 - t) * GROUP
            value = jnp.dot(lat[t], dec_all[first:first + window, off:off + wide],
                            preferred_element_type=jnp.float32)
            value = value + shift[:, off:off + wide]
            rec[t, :, off:off + wide] = value.astype(jnp.bfloat16)
            keep = jnp.logical_and(alone, s == t)
            to = rec_out.at[:, pl.ds(pl.multiple_of(h * half + off, 128), wide)]
            push_or_keep(rec.at[t, :, pl.ds(off, wide)], to, at_site(g, s, t),
                         base["rec"] + 2 * c + h, keep)

    for c in range(len(plan)):
        decode(c)

    for c, (off, wide) in enumerate(plan):
        for d in (0, 1):
            arrived(rec_out.at[:, pl.ds(d * half + off, wide)], base["rec"] + 2 * c + d)
    latents_copy.wait()
    for away, copy in pending:
        if away is None:
            copy.wait_send()
        else:
            pl.when(away)(copy.wait_send)


def on_device(acts, w_enc, b_enc, w_dec, b_dec):
    ring = lax.axis_size("tok")
    rows, width = acts.shape[1:]
    half = width // 2
    window = WINDOW * GROUP
    chunks = len(chunk_plan(half))
    blocks = WINDOW + 1
    hbm = pl.BlockSpec(memory_space=pl.ANY)
    vmem = pl.BlockSpec(memory_space=pltpu.VMEM)
    bf16, f32 = jnp.bfloat16, jnp.float32
    latents, recon = pl.pallas_call(
        functools.partial(kernel, ring),
        out_shape=(
            jax.ShapeDtypeStruct((rows, window), bf16),
            jax.ShapeDtypeStruct((rows, width), bf16),
        ),
        in_specs=[hbm, hbm, vmem, hbm, hbm],
        out_specs=(hbm, hbm),
        scratch_shapes=[
            pltpu.VMEM((2, rows, half), bf16),
            pltpu.VMEM((blocks * GROUP, half), bf16),
            pltpu.VMEM((blocks * GROUP, half), bf16),
            pltpu.VMEM((blocks, 8, 2 * GROUP), f32),
            pltpu.VMEM((2, 1, half), f32),
            pltpu.VMEM((2, rows, window), f32),
            pltpu.VMEM((rows, window), f32),
            pltpu.VMEM((rows, window), bf16),
            pltpu.VMEM((rows, window), bf16),
            pltpu.VMEM((rows, window), bf16),
            pltpu.VMEM((3, rows // 4, window), bf16),
            pltpu.VMEM((2, rows, window), bf16),
            pltpu.VMEM((2, rows, half), bf16),
            pltpu.SemaphoreType.DMA((40 + 6 * chunks,)),
            pltpu.SemaphoreType.DMA((sem_plan(chunks)[1],)),
        ],
        compiler_params=pltpu.CompilerParams(
            collective_id=0, has_side_effects=True, vmem_limit_bytes=40 * 1024 * 1024
        ),
        cost_estimate=pl.CostEstimate(
            flops=4 * rows * window * width, bytes_accessed=8 * rows * width, transcendentals=0
        ),
    )(acts[0], jnp.swapaxes(w_enc[0], 0, 1), b_enc.reshape(1, GROUP), w_dec[0], b_dec)
    return latents, recon[None]


def solution(mesh):
    return jax.shard_map(
        on_device,
        mesh=mesh,
        in_specs=(
            P("layer", "tok", None),
            P("layer", None, "tok"),
            P("tok"),
            P("layer", "tok", None),
            P("layer", None),
        ),
        out_specs=(P("tok", None), P("layer", "tok", None)),
        check_vma=False,
    )
```

time: 255 us -> 91.8 us (0.36)
  waiting for transfers between devices: 165 us -> 0 us
  Pallas kernels: 0 us -> 84.6 us
  starting transfers between devices: 45.6 us -> 0 us
  between operations: 14.3 us -> 0.65 us
  local copies, waits for them, and re-layouts: 15.1 us -> 6.26 us
  other arithmetic: 7.43 us -> 0 us
  matrix products: 5.95 us -> 0 us
    ppermute x21 -> x0, waiting for transfers between devices: 105 us -> none  [passed_along(): return lax.ppermute(value, axis, pairs)]
    pallas_call x0 -> x1, Pallas kernels: none -> 84.6 us  [on_device(): pl.pallas_call(functools.partial(kernel, ring), out_shape=(jax.ShapeDtype...]
    psum x1 -> x0, waiting for transfers between devices: 60.1 us -> none  [on_device(): lax.psum(partial_value.astype(jnp.bfloat16), 'layer').astype(jnp.float32)]
    ppermute x21 -> x0, starting transfers between devices: 45.5 us -> none  [passed_along(): return lax.ppermute(value, axis, pairs)]
    dot_general x2 -> x0, matrix products: 5.95 us -> none  [the longest x1 3.19 us: on_device(): partial_value = jnp.dot(rows, enc_cat, preferred_element_type=jnp.float32)]
    unnamed x19 -> x12, local copies, waits for them, and re-layouts: 12 us -> 6.26 us
    another operation x7 -> x0, other arithmetic: 3.75 us -> none  [on_device(): bias_stack = jnp.stack([p[2] for p in pieces])]
    convert_element_type x2 -> x0, other arithmetic: 2.95 us -> none  [the longest x1 1.78 us: on_device(): latents = jnp.maximum(pre + bias_all, 0.0).astype(jnp.bfloat16)]
  transfers between devices with their start and end apart: 22 -> 0, of which waited for: 20 -> 0; matrix products, arithmetic and copies ran while one was open for 9% -> 0% of each run, Pallas kernels for 0% -> 0%
where the time goes in v1:
time: 91.8 us; the launch traced here: 91.5 us
  Pallas kernels  84.6 us (92%)
  local copies, waits for them, and re-layouts  6.26 us (7%)
    pallas_call x1, Pallas kernels, on_device(): pl.pallas_call(functools.partial(kernel, ring), out_shape=(jax.ShapeDtype...  84.6 us
    unnamed x12, local copies, waits for them, and re-layouts  6.26 us

profile of v1, /device:TPU:1, one launch (start us, length us, event | category | flops | bytes accessed | tf_op | source)
XLA Modules:
  0.0 91.5 jit_solution(9089791784309539251)
XLA Ops:
  0.6 0.0 copy-start
  0.6 1.3 %copy-done = bf16[1,256,2304]{2,1,0:T(8,128)(2,1)S(1)} copy-done((bf16[1,256,2304]{2,1,0:T(8,128)(2,1)S(1)}, bf16[1,256,2304]{2,1,0:T(8,128)(2,1)}, u32[]{:S(2)}) %copy-start) | copy-done | bytes 1179672
  1.9 0.0 copy-start.1
  1.9 1.0 %copy-done.1 = bf16[1,2304,64]{1,2,0:T(8,128)(2,1)S(1)} copy-done((bf16[1,2304,64]{1,2,0:T(8,128)(2,1)S(1)}, bf16[1,2304,64]{1,2,0:T(8,128)(2,1)}, u32[]{:S(2)}) %copy-start.1) | copy-done | bytes 294936
  2.9 0.0 copy-start.2
  2.9 1.0 %copy-done.2 = bf16[1,64,2304]{2,1,0:T(8,128)(2,1)S(1)} copy-done((bf16[1,64,2304]{2,1,0:T(8,128)(2,1)S(1)}, bf16[1,64,2304]{2,1,0:T(8,128)(2,1)}, u32[]{:S(2)}) %copy-start.2) | copy-done | bytes 294936
  3.8 0.0 copy-start.3
  3.8 0.7 copy-done.3
  4.5 0.0 copy-start.4
  4.5 0.7 copy-done.4
  5.2 84.6 %shard_map.68 = (bf16[256,512]{1,0:T(8,128)(2,1)S(1)}, bf16[256,2304]{1,0:T(8,128)(2,1)S(1)}) custom-call(bf16[256,2304]{1,0:T(8,128)(2,1)S(1)} %bitcast.8, bf16[64,2304]{1,0:T(8,128)(2,1)S(1)} %bitcast.9, f32[1,64]{1,0:T(1,128)S(1)} %bitcast.11, bf16[64,2304]{1,0:T(8,128)(2,1)S(1)} %bitcast.10, f32[1,2304]{1,0:T(1,128)S(1)} %copy-done.3), custom_call_target="tpu_custom_call" | custom-call | flops 1207959552 | bytes 4718592 | tf_op jit(solution)/shard_map/pallas_call | solution.py:284
  89.8 0.7 copy.9
  90.5 1.0 %copy.10 = bf16[1,256,2304]{2,1,0:T(8,128)(2,1)} copy(bf16[1,256,2304]{2,1,0:T(8,128)(2,1)S(1)} %bitcast.7) | data formatting | bytes 2359296
Async XLA Ops:
  0.6 1.3 %copy-start = (bf16[1,256,2304]{2,1,0:T(8,128)(2,1)S(1)}, bf16[1,256,2304]{2,1,0:T(8,128)(2,1)}, u32[]{:S(2)}) copy-start(bf16[1,256,2304]{2,1,0:T(8,128)(2,1)} %param.5) | copy-start | bytes 3538948
  1.9 1.0 %copy-start.1 = (bf16[1,2304,64]{1,2,0:T(8,128)(2,1)S(1)}, bf16[1,2304,64]{1,2,0:T(8,128)(2,1)}, u32[]{:S(2)}) copy-start(bf16[1,2304,64]{1,2,0:T(8,128)(2,1)} %param.6) | copy-start | bytes 884740
  2.9 1.0 %copy-start.2 = (bf16[1,64,2304]{2,1,0:T(8,128)(2,1)S(1)}, bf16[1,64,2304]{2,1,0:T(8,128)(2,1)}, u32[]{:S(2)}) copy-start(bf16[1,64,2304]{2,1,0:T(8,128)(2,1)} %param.8) | copy-start | bytes 884740
  3.8 0.7 copy-start.3
  4.5 0.7 copy-start.4

commit v2 on v0

v2 whole, which is shorter than its diff:
```python
import functools

import jax
import jax.numpy as jnp
from jax import lax
from jax.experimental import pallas as pl
from jax.experimental.pallas import tpu as pltpu
from jax.sharding import PartitionSpec as P

GROUP = 64
WINDOW = 8
MESH = pl.DeviceIdType.MESH
ENC_WIDTHS = [640, 512]
DEC_WIDTHS = [384, 384, 384]


def column_plan(half, widths):
    if half != sum(widths):
        widths = [half]
    plan, at = [], 0
    for width in widths:
        plan.append((at, width))
        at += width
    return plan


def sem_plan(enc_pieces, dec_pieces):
    sizes = dict(own=2, enc=9 * enc_pieces, acts=2, bias=5, sib=2, part=6, gather=6, lat=8,
                 kept=1, half=2, dec=4 * dec_pieces, decx=4 * dec_pieces, out=1)
    at, plan = 0, {}
    for name, size in sizes.items():
        plan[name] = at
        at += size
    return plan, at


def kernel(ring, acts, enc, bias, dec, lat_out, dec_win,
           acts_all, enc_all, bias_all, pre, total, sib_out, sib_in,
           part_out, part_in, lat, send, recv):
    rows, width = acts.shape
    half = width // 2
    quarter = rows // 4
    window = WINDOW * GROUP
    part = window // 2
    enc_plan, dec_plan = column_plan(half, ENC_WIDTHS), column_plan(half, DEC_WIDTHS)
    base, _ = sem_plan(len(enc_plan), len(dec_plan))

    layer = lax.axis_index("layer")
    tok = lax.axis_index("tok")
    g, h = layer // 2, layer % 2
    m2, s = tok - tok % 2, tok % 2
    chip = 2 * g + s
    oh, os = 1 - h, 1 - s
    alone = h == s

    def at_site(g_, h_, s_):
        return (2 * g_ + h_, m2 + s_)

    following = (layer, lax.rem(tok + 2, ring))
    before = (layer, lax.rem(tok + ring - 2, ring))
    sibling = at_site(g, oh, s)
    across = at_site(g, h, os)

    pending = []

    def remote(src, dst, target, sem):
        return pltpu.make_async_remote_copy(
            src_ref=src, dst_ref=dst, send_sem=send.at[len(pending)], recv_sem=recv.at[sem],
            device_id=target, device_id_type=MESH)

    def push(src, dst, target, sem):
        copy = remote(src, dst, target, sem)
        copy.start()
        pending.append((None, copy))

    def push_if(cond, src, dst, target, sem):
        copy = remote(src, dst, target, sem)
        pl.when(cond)(copy.start)
        pending.append((cond, copy))

    def push_or_keep(src, dst, target, sem, keep):
        away = jnp.logical_not(keep)
        copy = remote(src, dst, target, sem)

        @pl.when(away)
        def _():
            copy.start()

        @pl.when(keep)
        def _():
            pltpu.make_async_copy(src, dst, recv.at[sem]).start()

        pending.append((away, copy))

    def arrived(dst, sem):
        pltpu.make_async_copy(dst, dst, recv.at[sem]).wait()

    def lanes(d):
        return pl.ds(pl.multiple_of(d * half, half), half)

    def block(b, count=1):
        if isinstance(b, int):
            return pl.ds(b * GROUP, count * GROUP)
        return pl.ds(pl.multiple_of(b * GROUP, GROUP), count * GROUP)

    own_bias = bias[...]
    bias_all[os] = jnp.broadcast_to(jnp.concatenate([own_bias, own_bias], axis=1), (8, 2 * GROUP))

    barrier = pltpu.get_barrier_semaphore()
    me = 2 * chip + h
    for j in range(1, 8):
        other = lax.rem(me + j, 8)
        pl.semaphore_signal(barrier, inc=1, device_id=at_site(other // 4, other % 2, (other // 2) % 2),
                            device_id_type=MESH)
    pl.semaphore_signal(barrier, inc=1, device_id=before, device_id_type=MESH)
    pl.semaphore_wait(barrier, 8)

    def exchange(src, dst, sem):
        push(src.at[:, lanes(oh)], dst, at_site(g, oh, h), sem)
        push_or_keep(src.at[:, lanes(h)], dst, at_site(g, h, h), sem, alone)

    pltpu.make_async_copy(dec, dec_win.at[block(os)], recv.at[base["kept"]]).start()
    exchange(enc, enc_all.at[block(os)], base["own"] + s)
    push(bias_all.at[os], bias_all.at[os], across, base["bias"])

    def enc_part(b, e):
        off, wide = enc_plan[e]
        return enc_all.at[block(b), pl.ds(off, wide)]

    def enc_wait(b, e):
        arrived(enc_part(b, e), base["enc"] + len(enc_plan) * b + e)

    def enc_send(b, e):
        push(enc_part(b, e), enc_part(b + 2, e), following, base["enc"] + len(enc_plan) * (b + 2) + e)

    def enc_pass(b):
        for e in range(len(enc_plan)):
            enc_wait(b, e)
            enc_send(b, e)

    def enc_own(b, p):
        arrived(enc_all.at[block(b)], base["own"] + p)
        for e in range(len(enc_plan)):
            enc_send(b, e)

    def bias_pass(i):
        if i == 0:
            arrived(bias_all.at[s], base["bias"])
        else:
            arrived(bias_all.at[pl.ds(2 * i, 2)], base["bias"] + i)
        count = 1 if i == 3 else 2
        push(bias_all.at[pl.ds(2 * i, count)], bias_all.at[pl.ds(2 * i + 2, count)], following,
             base["bias"] + i + 1)

    enc_own(os, s)
    enc_own(s, os)
    push(dec.at[:, lanes(os)], dec_win.at[block(os), lanes(os)], across, base["half"])
    exchange(acts, acts_all.at[s], base["acts"] + s)
    push_if(s == 0, dec.at[:, lanes(0)], dec_win.at[block(1), lanes(0)], across, base["half"] + 1)
    bias_pass(0)

    for i in (1, 2):
        enc_pass(2 * i + os)
        enc_pass(2 * i + s)
        bias_pass(i)
    enc_pass(6)
    bias_pass(3)

    def columns(q):
        return pl.ds(q * part, part)

    def encode(t, q):
        first = (1 - t) * GROUP + q * part
        pre[t, :, q * part:(q + 1) * part] = lax.dot_general(
            acts_all[t], enc_all[first:first + part, :], (((1,), (1,)), ((), ())),
            preferred_element_type=jnp.float32)

    def cores_send(q):
        sib_out[q] = pre[oh, :, q * part:(q + 1) * part].astype(jnp.bfloat16)
        push(sib_out.at[q], sib_in.at[q], sibling, base["sib"] + q)

    def chip_rows(c_):
        return pl.ds(pl.multiple_of(c_ * quarter, quarter), quarter)

    def chips_send(q):
        arrived(sib_in.at[q], base["sib"] + q)
        value = pre[h, :, q * part:(q + 1) * part] + sib_in[q].astype(jnp.float32)
        total[:, q * part:(q + 1) * part] = value
        part_out[:, q * part:(q + 1) * part] = value.astype(jnp.bfloat16)
        for j in (2, 1, 3):
            other = lax.rem(chip + j, 4)
            push(part_out.at[chip_rows(other), columns(q)], part_in.at[3 * q + j - 1],
                 at_site(other // 2, h, other % 2), base["part"] + 3 * q + j - 1)

    def latents_send(q):
        value = total[chip_rows(chip), q * part:(q + 1) * part] + bias_row[:, q * part:(q + 1) * part]
        for j in (1, 3, 2):
            arrived(part_in.at[3 * q + j - 1], base["part"] + 3 * q + j - 1)
            value = value + part_in[3 * q + j - 1].astype(jnp.float32)
        lat[h, chip_rows(chip), q * part:(q + 1) * part] = jnp.maximum(value, 0.0).astype(jnp.bfloat16)
        mine = lat.at[h, chip_rows(chip), columns(q)]
        for j in (2, 1, 3):
            other = lax.rem(chip + j, 4)
            push(mine, mine, at_site(other // 2, h, other % 2), base["gather"] + 3 * q + j - 1)
        push(mine, mine, sibling, base["lat"] + 4 * q)

    def latents_share(q):
        for j in (1, 3, 2):
            piece = lat.at[h, chip_rows(lax.rem(chip + 4 - j, 4)), columns(q)]
            arrived(piece, base["gather"] + 3 * q + j - 1)
            push(piece, piece, sibling, base["lat"] + 4 * q + j)

    def latents_wait(q):
        for j in (0, 1, 3, 2):
            arrived(lat.at[oh, chip_rows(lax.rem(chip + 4 - j, 4)), columns(q)], base["lat"] + 4 * q + j)

    def dec_part(b, count, c, side):
        off, wide = dec_plan[c]
        return dec_win.at[pl.ds(b * GROUP, count * GROUP),
                          pl.ds(pl.multiple_of(side * half + off, 128), wide)]

    def dec_sem(kind, i, c):
        return base[kind] + len(dec_plan) * (i - 1) + c

    def dec_pass(i):
        count = 1 if i == 3 else 2
        for c in range(len(dec_plan)):
            if i > 0:
                arrived(dec_part(2 * i, 2, c, s), dec_sem("dec", i, c))
            push(dec_part(2 * i, count, c, s), dec_part(2 * i + 2, count, c, s), following,
                 dec_sem("dec", i + 1, c))
            if i > 0:
                push(dec_part(2 * i, 2, c, s), dec_part(2 * i, 2, c, s), across, dec_sem("decx", i, c))

    arrived(dec_win.at[block(os)], base["kept"])
    arrived(dec_win.at[block(s), lanes(s)], base["half"])
    dec_pass(0)

    arrived(acts_all.at[0], base["acts"])
    arrived(acts_all.at[1], base["acts"] + 1)
    encode(1, 0)
    encode(0, 0)
    cores_send(0)
    for e in range(len(enc_plan)):
        enc_wait(7, e)
    encode(1, 1)
    arrived(bias_all.at[pl.ds(8, 1)], base["bias"] + 4)
    low = lax.broadcasted_iota(jnp.int32, (1, 2 * GROUP), 1) < GROUP
    bias_row = jnp.concatenate(
        [jnp.where(low, bias_all[oh + k, 0:1, :], bias_all[oh + k + 1, 0:1, :])
         for k in range(0, WINDOW, 2)], axis=1)
    chips_send(0)
    for e in range(len(enc_plan)):
        enc_wait(8, e)
    encode(0, 1)
    cores_send(1)
    dec_pass(1)
    chips_send(1)
    latents_send(0)
    dec_pass(2)
    latents_send(1)
    latents_share(0)
    dec_pass(3)
    latents_share(1)
    latents_wait(0)
    latents_wait(1)
    latents_copy = pltpu.make_async_copy(lat.at[s], lat_out, recv.at[base["out"]])
    latents_copy.start()
    for c in range(len(dec_plan)):
        arrived(dec_part(8, 1, c, s), dec_sem("dec", 4, c))
        push_if(s == 1, dec_part(8, 1, c, 1), dec_part(8, 1, c, 1), across, dec_sem("decx", 4, c))

    @pl.when(s == 1)
    def _():
        arrived(dec_win.at[block(1), lanes(0)], base["half"] + 1)

    for i in (1, 2, 3):
        for c in range(len(dec_plan)):
            arrived(dec_part(2 * i, 2, c, os), dec_sem("decx", i, c))

    @pl.when(s == 0)
    def _():
        for c in range(len(dec_plan)):
            arrived(dec_part(8, 1, c, 1), dec_sem("decx", 4, c))

    latents_copy.wait()
    for away, copy in pending:
        if away is None:
            copy.wait_send()
        else:
            pl.when(away)(copy.wait_send)


def decode(lat, dec_win, bdec, lat_out, rec_out):
    first = pl.multiple_of((1 - lax.axis_index("tok") % 2) * GROUP, GROUP)
    value = jnp.dot(lat[...], dec_win[pl.ds(first, lat.shape[1]), :], preferred_element_type=jnp.float32)
    rec_out[...] = (value + bdec[...]).astype(jnp.bfloat16)

    @pl.when(pl.program_id(0) == 0)
    def _():
        lat_out[...] = lat[...]


def on_device(acts, w_enc, b_enc, w_dec, b_dec):
    ring = lax.axis_size("tok")
    rows, width = acts.shape[1:]
    half = width // 2
    window = WINDOW * GROUP
    blocks = WINDOW + 1
    _, arrivals = sem_plan(len(column_plan(half, ENC_WIDTHS)), len(column_plan(half, DEC_WIDTHS)))
    hbm = pl.BlockSpec(memory_space=pl.ANY)
    vmem = pl.BlockSpec(memory_space=pltpu.VMEM)
    bf16, f32 = jnp.bfloat16, jnp.float32
    latents, dec_win = pl.pallas_call(
        functools.partial(kernel, ring),
        out_shape=(
            jax.ShapeDtypeStruct((rows, window), bf16),
            jax.ShapeDtypeStruct((blocks * GROUP, width), bf16),
        ),
        in_specs=[hbm, hbm, vmem, hbm],
        out_specs=(hbm, hbm),
        scratch_shapes=[
            pltpu.VMEM((2, rows, half), bf16),
            pltpu.VMEM((blocks * GROUP, half), bf16),
            pltpu.VMEM((blocks, 8, 2 * GROUP), f32),
            pltpu.VMEM((2, rows, window), f32),
            pltpu.VMEM((rows, window), f32),
            pltpu.VMEM((2, rows, window // 2), bf16),
            pltpu.VMEM((2, rows, window // 2), bf16),
            pltpu.VMEM((rows, window), bf16),
            pltpu.VMEM((6, rows // 4, window // 2), bf16),
            pltpu.VMEM((2, rows, window), bf16),
            pltpu.SemaphoreType.DMA((80,)),
            pltpu.SemaphoreType.DMA((arrivals,)),
        ],
        compiler_params=pltpu.CompilerParams(
            collective_id=0, has_side_effects=True, vmem_limit_bytes=60 * 1024 * 1024
        ),
        cost_estimate=pl.CostEstimate(
            flops=2 * rows * window * width, bytes_accessed=8 * rows * width, transcendentals=0
        ),
    )(acts[0], jnp.swapaxes(w_enc[0], 0, 1), b_enc.reshape(1, GROUP), w_dec[0])
    steps = 3 if width % 384 == 0 else 1
    wide = width // steps
    latents, recon = pl.pallas_call(
        decode,
        grid=(steps,),
        out_shape=(
            jax.ShapeDtypeStruct((rows, window), bf16),
            jax.ShapeDtypeStruct((rows, width), bf16),
        ),
        in_specs=[
            pl.BlockSpec((rows, window), lambda i: (0, 0)),
            pl.BlockSpec((blocks * GROUP, wide), lambda i: (0, i)),
            pl.BlockSpec((1, wide), lambda i: (0, i)),
        ],
        out_specs=(
            pl.BlockSpec((rows, window), lambda i: (0, 0)),
            pl.BlockSpec((rows, wide), lambda i: (0, i)),
        ),
        cost_estimate=pl.CostEstimate(
            flops=2 * rows * window * width, bytes_accessed=6 * rows * width, transcendentals=0
        ),
    )(latents, dec_win, b_dec)
    return latents, recon[None]


def solution(mesh):
    return jax.shard_map(
        on_device,
        mesh=mesh,
        in_specs=(
            P("layer", "tok", None),
            P("layer", None, "tok"),
            P("tok"),
            P("layer", "tok", None),
            P("layer", None),
        ),
        out_specs=(P("tok", None), P("layer", "tok", None)),
        check_vma=False,
    )
```

time: 255 us -> 86.7 us (0.34)
  waiting for transfers between devices: 165 us -> 0 us
  Pallas kernels: 0 us -> 85.9 us
  starting transfers between devices: 45.6 us -> 0 us
  local copies, waits for them, and re-layouts: 15.1 us -> 0 us
  between operations: 14.3 us -> 0.64 us
  other arithmetic: 7.43 us -> 0 us
  matrix products: 5.95 us -> 0 us
    ppermute x21 -> x0, waiting for transfers between devices: 105 us -> none  [passed_along(): return lax.ppermute(value, axis, pairs)]
    pallas_call x0 -> x2, Pallas kernels: none -> 85.9 us  [the longest x1 81.7 us: on_device(): pl.pallas_call(functools.partial(kernel, ring), out_shape=(jax.ShapeDtype...]
    psum x1 -> x0, waiting for transfers between devices: 60.1 us -> none  [on_device(): lax.psum(partial_value.astype(jnp.bfloat16), 'layer').astype(jnp.float32)]
    ppermute x21 -> x0, starting transfers between devices: 45.5 us -> none  [passed_along(): return lax.ppermute(value, axis, pairs)]
    unnamed x19 -> x0, local copies, waits for them, and re-layouts: 12 us -> none
    dot_general x2 -> x0, matrix products: 5.95 us -> none  [the longest x1 3.19 us: on_device(): partial_value = jnp.dot(rows, enc_cat, preferred_element_type=jnp.float32)]
    another operation x7 -> x0, other arithmetic: 3.75 us -> none  [on_device(): bias_stack = jnp.stack([p[2] for p in pieces])]
    convert_element_type x2 -> x0, other arithmetic: 2.95 us -> none  [the longest x1 1.78 us: on_device(): latents = jnp.maximum(pre + bias_all, 0.0).astype(jnp.bfloat16)]
  transfers between devices with their start and end apart: 22 -> 0, of which waited for: 20 -> 0; matrix products, arithmetic and copies ran while one was open for 9% -> 0% of each run, Pallas kernels for 0% -> 0%
where the time goes in v2:
time: 86.7 us; the launch traced here: 86.5 us
  Pallas kernels  85.9 us (99%)
    pallas_call x1, Pallas kernels, on_device(): pl.pallas_call(functools.partial(kernel, ring), out_shape=(jax.ShapeDtype...  81.7 us
    pallas_call x1, Pallas kernels, on_device(): pl.pallas_call(decode, grid=(steps,), out_shape=(jax.ShapeDtypeStruct((ro...  4.18 us

profile of v2, /device:TPU:1, one launch (start us, length us, event | category | flops | bytes accessed | tf_op | source)
XLA Modules:
  0.0 86.5 jit_solution(10165841787096501384)
XLA Ops:
  0.6 81.7 %shard_map.68 = (bf16[256,512]{1,0:T(8,128)(2,1)}, bf16[576,2304]{1,0:T(8,128)(2,1)}) custom-call(bf16[256,2304]{1,0:T(8,128)(2,1)} %bitcast.7, bf16[64,2304]{1,0:T(8,128)(2,1)} %bitcast.9, f32[1,64]{1,0:T(1,128)} %bitcast.11, bf16[64,2304]{1,0:T(8,128)(2,1)} %bitcast.10), custom_call_target="tpu_custom_call" | custom-call | flops 603979776 | bytes 4718592 | tf_op jit(solution)/shard_map/pallas_call | solution.py:314
  82.3 4.2 %shard_map.69 = (bf16[256,512]{1,0:T(8,128)(2,1)}, bf16[256,2304]{1,0:T(8,128)(2,1)}) custom-call(bf16[256,512]{1,0:T(8,128)(2,1)} %get-tuple-element.6.lat, bf16[576,2304]{1,0:T(8,128)(2,1)} %get-tuple-element.7.dec_win, f32[1,2304]{1,0:T(1,128)} %bdec.1), custom_call_target="tpu_custom_call" | custom-call | flops 603979776 | bytes 3538944 | tf_op jit(solution)/shard_map/pallas_call | solution.py:345

commit v3 on v2

--- a/solution.py
+++ b/solution.py
@@ -68,6 +68,16 @@
             src_ref=src, dst_ref=dst, send_sem=send.at[len(pending)], recv_sem=recv.at[sem],
             device_id=target, device_id_type=MESH)
 
+    settled = [0]
+
+    def settle(count):
+        for away, copy in pending[settled[0]:count]:
+            if away is None:
+                copy.wait_send()
+            else:
+                pl.when(away)(copy.wait_send)
+        settled[0] = max(settled[0], count)
+
     def push(src, dst, target, sem):
         copy = remote(src, dst, target, sem)
         copy.start()
@@ -138,10 +148,18 @@
             enc_wait(b, e)
             enc_send(b, e)
 
-    def enc_own(b, p):
+    def enc_own(b, p, near):
+        sem = base["enc"] + len(enc_plan) * (b + 2)
+        if near:
+            for e, (off, wide) in enumerate(enc_plan):
+                here = enc.at[:, pl.ds(pl.multiple_of(h * half + off, 128), wide)]
+                push_if(alone, here, enc_part(b + 2, e), following, sem + e)
         arrived(enc_all.at[block(b)], base["own"] + p)
         for e in range(len(enc_plan)):
-            enc_send(b, e)
+            if near:
+                push_if(jnp.logical_not(alone), enc_part(b, e), enc_part(b + 2, e), following, sem + e)
+            else:
+                enc_send(b, e)
 
     def bias_pass(i):
         if i == 0:
@@ -152,8 +170,8 @@
         push(bias_all.at[pl.ds(2 * i, count)], bias_all.at[pl.ds(2 * i + 2, count)], following,
              base["bias"] + i + 1)
 
-    enc_own(os, s)
-    enc_own(s, os)
+    enc_own(os, s, True)
+    enc_own(s, os, False)
     push(dec.at[:, lanes(os)], dec_win.at[block(os), lanes(os)], across, base["half"])
     exchange(acts, acts_all.at[s], base["acts"] + s)
     push_if(s == 0, dec.at[:, lanes(0)], dec_win.at[block(1), lanes(0)], across, base["half"] + 1)
@@ -222,9 +240,9 @@
     def dec_sem(kind, i, c):
         return base[kind] + len(dec_plan) * (i - 1) + c
 
-    def dec_pass(i):
+    def dec_pass(i, pieces=range(len(dec_plan))):
         count = 1 if i == 3 else 2
-        for c in range(len(dec_plan)):
+        for c in pieces:
             if i > 0:
                 arrived(dec_part(2 * i, 2, c, s), dec_sem("dec", i, c))
             push(dec_part(2 * i, count, c, s), dec_part(2 * i + 2, count, c, s), following,
@@ -254,14 +272,21 @@
         enc_wait(8, e)
     encode(0, 1)
     cores_send(1)
-    dec_pass(1)
+    sent = len(pending)
+    dec_pass(1, [0])
     chips_send(1)
+    dec_pass(1, [1])
     latents_send(0)
-    dec_pass(2)
+    dec_pass(1, range(2, len(dec_plan)))
     latents_send(1)
     latents_share(0)
+    dec_pass(2, [0])
+    dec_pass(2, [1])
+    latents_share(1)
+    dec_pass(2, range(2, len(dec_plan)))
+    settle(sent)
+    sent = len(pending)
     dec_pass(3)
-    latents_share(1)
     latents_wait(0)
     latents_wait(1)
     latents_copy = pltpu.make_async_copy(lat.at[s], lat_out, recv.at[base["out"]])
@@ -269,6 +294,7 @@
     for c in range(len(dec_plan)):
         arrived(dec_part(8, 1, c, s), dec_sem("dec", 4, c))
         push_if(s == 1, dec_part(8, 1, c, 1), dec_part(8, 1, c, 1), across, dec_sem("decx", 4, c))
+    settle(sent)
 
     @pl.when(s == 1)
     def _():
@@ -284,21 +310,38 @@
             arrived(dec_part(8, 1, c, 1), dec_sem("decx", 4, c))
 
     latents_copy.wait()
-    for away, copy in pending:
-        if away is None:
-            copy.wait_send()
-        else:
-            pl.when(away)(copy.wait_send)
-
-
-def decode(lat, dec_win, bdec, lat_out, rec_out):
+    settle(len(pending))
+
+
+def decode(lat, dec_win, bdec, lat_out, rec_out, lat_here, win_here, bias_here, rec_here, came, left):
+    window = lat.shape[1]
     first = pl.multiple_of((1 - lax.axis_index("tok") % 2) * GROUP, GROUP)
-    value = jnp.dot(lat[...], dec_win[pl.ds(first, lat.shape[1]), :], preferred_element_type=jnp.float32)
-    rec_out[...] = (value + bdec[...]).astype(jnp.bfloat16)
-
-    @pl.when(pl.program_id(0) == 0)
-    def _():
-        lat_out[...] = lat[...]
+    steps = came.shape[0] - 2
+    wide = dec_win.shape[1] // steps
+
+    def columns(c):
+        return pl.ds(c * wide, wide)
+
+    coming = [pltpu.make_async_copy(lat, lat_here, came.at[0]), pltpu.make_async_copy(bdec, bias_here, came.at[1])]
+    for c in range(steps):
+        coming.append(pltpu.make_async_copy(dec_win.at[pl.ds(first, window), columns(c)],
+                                            win_here.at[:, columns(c)], came.at[2 + c]))
+    for copy in coming:
+        copy.start()
+    coming[0].wait()
+    leaving = [pltpu.make_async_copy(lat_here, lat_out, left.at[0])]
+    leaving[0].start()
+    coming[1].wait()
+    for c in range(steps):
+        at = slice(c * wide, (c + 1) * wide)
+        coming[2 + c].wait()
+        value = jnp.dot(lat_here[...], win_here[:, at], preferred_element_type=jnp.float32)
+        rec_here[:, at] = (value + bias_here[:, at]).astype(jnp.bfloat16)
+        leaving.append(pltpu.make_async_copy(rec_here.at[:, columns(c)], rec_out.at[:, columns(c)],
+                                             left.at[1 + c]))
+        leaving[-1].start()
+    for copy in leaving:
+        copy.wait()
 
 
 def on_device(acts, w_enc, b_enc, w_dec, b_dec):
@@ -340,24 +383,24 @@
             flops=2 * rows * window * width, bytes_accessed=8 * rows * width, transcendentals=0
         ),
     )(acts[0], jnp.swapaxes(w_enc[0], 0, 1), b_enc.reshape(1, GROUP), w_dec[0])
-    steps = 3 if width % 384 == 0 else 1
-    wide = width // steps
+    steps = 6 if width % 768 == 0 else 1
     latents, recon = pl.pallas_call(
         decode,
-        grid=(steps,),
         out_shape=(
             jax.ShapeDtypeStruct((rows, window), bf16),
             jax.ShapeDtypeStruct((rows, width), bf16),
         ),
-        in_specs=[
-            pl.BlockSpec((rows, window), lambda i: (0, 0)),
-            pl.BlockSpec((blocks * GROUP, wide), lambda i: (0, i)),
-            pl.BlockSpec((1, wide), lambda i: (0, i)),
+        in_specs=[hbm, hbm, hbm],
+        out_specs=(hbm, hbm),
+        scratch_shapes=[
+            pltpu.VMEM((rows, window), bf16),
+            pltpu.VMEM((window, width), bf16),
+            pltpu.VMEM((1, width), f32),
+            pltpu.VMEM((rows, width), bf16),
+            pltpu.SemaphoreType.DMA((steps + 2,)),
+            pltpu.SemaphoreType.DMA((steps + 1,)),
         ],
-        out_specs=(
-            pl.BlockSpec((rows, window), lambda i: (0, 0)),
-            pl.BlockSpec((rows, wide), lambda i: (0, i)),
-        ),
+        compiler_params=pltpu.CompilerParams(vmem_limit_bytes=60 * 1024 * 1024),
         cost_estimate=pl.CostEstimate(
             flops=2 * rows * window * width, bytes_accessed=6 * rows * width, transcendentals=0
         ),

time: 86.7 us -> 84.6 us (0.976)
  Pallas kernels: 85.9 us -> 83.8 us
    pallas_call x1, Pallas kernels: 81.7 us -> 80.1 us  [on_device(): pl.pallas_call(functools.partial(kernel, ring), out_shape=(jax.ShapeDtype...]
where the time goes in v3:
time: 84.6 us; the launch traced here: 84.4 us
  Pallas kernels  83.8 us (99%)
    pallas_call x1, Pallas kernels, on_device(): pl.pallas_call(functools.partial(kernel, ring), out_shape=(jax.ShapeDtype...  80.1 us
    pallas_call x1, Pallas kernels, on_device(): pl.pallas_call(decode, out_shape=(jax.ShapeDtypeStruct((rows, window), bf...  3.7 us

profile of v3, /device:TPU:1, one launch (start us, length us, event | category | flops | bytes accessed | tf_op | source)
XLA Modules:
  0.0 84.4 jit_solution(2510521268596006961)
XLA Ops:
  0.6 80.1 %shard_map.68 = (bf16[256,512]{1,0:T(8,128)(2,1)}, bf16[576,2304]{1,0:T(8,128)(2,1)}) custom-call(bf16[256,2304]{1,0:T(8,128)(2,1)} %bitcast.7, bf16[64,2304]{1,0:T(8,128)(2,1)} %bitcast.9, f32[1,64]{1,0:T(1,128)} %bitcast.11, bf16[64,2304]{1,0:T(8,128)(2,1)} %bitcast.10), custom_call_target="tpu_custom_call" | custom-call | flops 603979776 | bytes 4718592 | tf_op jit(solution)/shard_map/pallas_call | solution.py:357
  80.7 3.7 %shard_map.69 = (bf16[256,512]{1,0:T(8,128)(2,1)}, bf16[256,2304]{1,0:T(8,128)(2,1)}) custom-call(bf16[256,512]{1,0:T(8,128)(2,1)} %get-tuple-element.6.lat, bf16[576,2304]{1,0:T(8,128)(2,1)} %get-tuple-element.7.dec_win, f32[1,2304]{1,0:T(1,128)} %bdec.1), custom_call_target="tpu_custom_call" | custom-call | flops 603979776 | bytes 3538944 | tf_op jit(solution)/shard_map/pallas_call | solution.py:387

commit v4 on v3

--- a/solution.py
+++ b/solution.py
@@ -10,8 +10,8 @@
 GROUP = 64
 WINDOW = 8
 MESH = pl.DeviceIdType.MESH
-ENC_WIDTHS = [640, 512]
-DEC_WIDTHS = [384, 384, 384]
+ENC_WIDTHS = [1152]
+DEC_WIDTHS = [512, 384, 256]
 
 
 def column_plan(half, widths):

time: 84.6 us -> 85.9 us (1.015)
  Pallas kernels: 83.8 us -> 85.1 us
    pallas_call x1, Pallas kernels: 80.1 us -> 81.4 us  [on_device(): pl.pallas_call(functools.partial(kernel, ring), out_shape=(jax.ShapeDtype...]
where the time goes in v4:
time: 85.9 us; the launch traced here: 85.7 us
  Pallas kernels  85.1 us (99%)
    pallas_call x1, Pallas kernels, on_device(): pl.pallas_call(functools.partial(kernel, ring), out_shape=(jax.ShapeDtype...  81.4 us
    pallas_call x1, Pallas kernels, on_device(): pl.pallas_call(decode, out_shape=(jax.ShapeDtypeStruct((rows, window), bf...  3.71 us

profile of v4, /device:TPU:1, one launch (start us, length us, event | category | flops | bytes accessed | tf_op | source)
XLA Modules:
  0.0 85.7 jit_solution(11545257395427870991)
XLA Ops:
  0.6 81.4 %shard_map.68 = (bf16[256,512]{1,0:T(8,128)(2,1)}, bf16[576,2304]{1,0:T(8,128)(2,1)}) custom-call(bf16[256,2304]{1,0:T(8,128)(2,1)} %bitcast.7, bf16[64,2304]{1,0:T(8,128)(2,1)} %bitcast.9, f32[1,64]{1,0:T(1,128)} %bitcast.11, bf16[64,2304]{1,0:T(8,128)(2,1)} %bitcast.10), custom_call_target="tpu_custom_call" | custom-call | flops 603979776 | bytes 4718592 | tf_op jit(solution)/shard_map/pallas_call | solution.py:357
  82.0 3.7 %shard_map.69 = (bf16[256,512]{1,0:T(8,128)(2,1)}, bf16[256,2304]{1,0:T(8,128)(2,1)}) custom-call(bf16[256,512]{1,0:T(8,128)(2,1)} %get-tuple-element.6.lat, bf16[576,2304]{1,0:T(8,128)(2,1)} %get-tuple-element.7.dec_win, f32[1,2304]{1,0:T(1,128)} %bdec.1), custom_call_target="tpu_custom_call" | custom-call | flops 603979776 | bytes 3538944 | tf_op jit(solution)/shard_map/pallas_call | solution.py:387
